TPU v7x, 128 devices: a whole 4x4x4 slice. The times are simulated.
128 devices in a mesh: replica: 16 (over x_hi, z, core), group: 8 (over y, x_lo).
Axes of the slice: x: 4 (x_hi: 2, x_lo: 2; x = x_hi * 2 + x_lo), y: 4, z: 4, core: 2. Of those that a mesh axis runs over, the one named last changes fastest.
Arguments:
- tokens: bfloat16 [16384, 960], P(('replica', 'group')), may hold values from -6 to 6
- cotangent: bfloat16 [16384, 960], P(('replica', 'group')), may hold values from -6 to 6
- lengths: int32 [128, 3], P(('replica', 'group')), may hold values from 1 to 64, 128 in all within a row
- gain_attn: bfloat16 [2, 960], P(None, 'group'), may hold values from 0.5 to 1.5
- w_query: bfloat16 [2, 960, 960], P(None, 'group'), may hold values from -0.1875 to 0.1875
- w_key: bfloat16 [2, 960, 320], P(None, 'group'), may hold values from -0.1875 to 0.1875
- w_value: bfloat16 [2, 960, 320], P(None, 'group'), may hold values from -0.1875 to 0.1875
- w_out: bfloat16 [2, 960, 960], P(None, 'group'), may hold values from -1.5 to 1.5
- gain_mlp: bfloat16 [2, 960], P(None, 'group'), may hold values from 0.5 to 1.5
- w_gate: bfloat16 [2, 960, 2560], P(None, None, 'group'), may hold values from -0.1875 to 0.1875
- w_up: bfloat16 [2, 960, 2560], P(None, None, 'group'), may hold values from -0.1875 to 0.1875
- w_down: bfloat16 [2, 2560, 960], P(None, 'group'), may hold values from -0.125 to 0.125
Outputs:
- activations: bfloat16 [16384, 960], P(('replica', 'group'))
- grad_tokens: float32 [16384, 960], P(('replica', 'group'))
- grad_gain_attn: float32 [2, 960], P(None, 'group')
- grad_w_query: float32 [2, 960, 960], P(None, 'group')
- grad_w_key: float32 [2, 960, 320], P(None, 'group')
- grad_w_value: float32 [2, 960, 320], P(None, 'group')
- grad_w_out: float32 [2, 960, 960], P(None, 'group')
- grad_gain_mlp: float32 [2, 960], P(None, 'group')
- grad_w_gate: float32 [2, 960, 2560], P(None, None, 'group')
- grad_w_up: float32 [2, 960, 2560], P(None, None, 'group')
- grad_w_down: float32 [2, 2560, 960], P(None, 'group')
Inputs may be any that keep to these rules, and one draw needn't show every extreme that they name: Each row holds the lengths of 3 sequences that fill one device's 128 tokens in order; one of them is exactly 64 long.
All inputs are finite; a program needn't handle non-finite values.
Results may differ from a plain program's by a relative error of at most 0.03.
Values may be sent and summed in bfloat16 or wider, within the bound.
A program may use at most 192 MiB of HBM per device.

v0:
```python
import jax
import jax.numpy as jnp
from jax import lax
from jax.experimental import pallas as pl
from jax.experimental.pallas import tpu as pltpu
from jax.sharding import PartitionSpec as P

Q_HEADS = 15
KV_HEADS = 5
HEAD = 64
LAYERS = 2
D = 960
SHARD = 120
PAD = 128
FFS = 320
ROWS = 128
KV = KV_HEADS * HEAD
SHARE = Q_HEADS // KV_HEADS

norm_eps = 1e-05
rope_base = 100000.0
log_base = 11.512925464970229
score_scale = 0.125
masked_value = -1e30
MESH = pl.DeviceIdType.MESH
BF = jnp.bfloat16
F32 = jnp.float32
ANY = pl.BlockSpec(memory_space=pl.ANY)
VMEM = pl.BlockSpec(memory_space=pltpu.VMEM)
SMEM = pl.BlockSpec(memory_space=pltpu.SMEM)


def coords():
    r = lax.axis_index("replica")
    g = lax.axis_index("group")
    return r // 8, (r // 2) % 4, r % 2, g // 2, g % 2


def device(x_hi, z, core, y, x_lo):
    return ((x_hi * 4 + z) * 2 + core, y * 2 + x_lo)


def remote(src, dst, sems, index, target):
    return pltpu.make_async_remote_copy(
        src_ref=src,
        dst_ref=dst,
        send_sem=sems[0].at[index],
        recv_sem=sems[1].at[index],
        device_id=target,
        device_id_type=MESH,
    )


def dot(a, b):
    return lax.dot_general(a, b, (((1,), (0,)), ((), ())), preferred_element_type=F32)


def dot_t(a, b):
    return lax.dot_general(a, b, (((1,), (1,)), ((), ())), preferred_element_type=F32)


def t_dot(a, b):
    return lax.dot_general(a, b, (((0,), (0,)), ((), ())), preferred_element_type=F32)


def lanes(g, width):
    return pl.ds(pl.multiple_of(g * PAD, PAD), width)


def halves(a):
    high = a.astype(BF)
    return high, (a - high.astype(F32)).astype(BF)


def accumulate(dst, others, chunk):
    def body(i, carry):
        at = pl.ds(pl.multiple_of(i * chunk, chunk), chunk)
        total = dst[at, :].astype(F32)
        for other in others:
            total = total + other[at, :].astype(F32)
        dst[at, :] = total.astype(dst.dtype)
        return carry

    lax.fori_loop(0, dst.shape[0] // chunk, body, 0)


class Slots:
    def __init__(self):
        self.used = 0

    def take(self, count=1):
        self.used += count
        return self.used - count


def order(k):
    return k + (k // 2) * (5 - 2 * k)


KINDS = {
    "m": ((3, FFS, D), False),
    "o": ((1, ROWS, D), True),
    "q": ((1, ROWS, D), True),
    "kv": ((2, KV, PAD), True),
}
TWICE = ("q", "kv")
SUMS_TWICE = ("o", "q", "kv")
ORDER_Y = (1, 3, 2)


def quarter(shape):
    return (shape[0], shape[1] // 4, shape[2])


def scratch_shapes():
    L = LAYERS
    named = {}

    def buf(name, *shape, dtype=BF):
        named[name] = pltpu.VMEM(shape, dtype)

    buf("aq", 4, 2, SHARD, D)
    buf("ao", 4, 2, SHARD, D)
    buf("ak", 4, 2, KV, SHARD)
    buf("av", 4, 2, KV, SHARD)
    buf("mw", 2, 3, FFS, D)
    buf("all_gains", 4, 2, 16, PAD)
    buf("own_gains", 16, PAD)
    buf("place", D, 8 * PAD)
    buf("cosine", ROWS, PAD, dtype=F32)
    buf("sine", ROWS, PAD, dtype=F32)
    buf("bias", ROWS, ROWS, dtype=F32)
    buf("gain_full", 16, D, dtype=F32)
    buf("gain_pad", 16, 8 * PAD)
    buf("gain_grad", 16, 8 * PAD, dtype=F32)
    buf("gain_rows", 16, D, dtype=F32)
    buf("stream", L, ROWS, D, dtype=F32)
    buf("hidden", L, ROWS, D, dtype=F32)
    buf("grad", ROWS, D, dtype=F32)
    buf("wide", ROWS, 8 * PAD, dtype=F32)
    buf("narrow", ROWS, 3 * PAD, dtype=F32)
    buf("own_part", ROWS, D, dtype=F32)
    buf("npad", L, ROWS, 8 * PAD)
    buf("mpad", L, ROWS, 8 * PAD)
    buf("qrot", L, ROWS, 8 * PAD)
    buf("krot", L, ROWS, 3 * PAD)
    buf("vals", L, ROWS, 3 * PAD)
    buf("gproj_q", ROWS, 8 * PAD)
    buf("gproj_k", ROWS, 3 * PAD)
    buf("gproj_v", ROWS, 3 * PAD)
    buf("gmix", ROWS, D)
    buf("glow", ROWS, D)
    buf("acts_in", L, 4, ROWS, D)
    buf("grads_in", 2, 4, ROWS, D)
    buf("parts", 2, 3, ROWS, D)
    buf("came", 2, 3, ROWS, D)
    buf("s_gate", L, 2, 4, ROWS, FFS)
    buf("s_up", L, 2, 4, ROWS, FFS)
    buf("s_act", L, 2, 4, ROWS, FFS)
    for kind, (shape, spread) in KINDS.items():
        four = (4,) if spread else ()
        copies = L if kind in TWICE else 1
        if kind != "o":
            buf("g_" + kind, *four, 2, *shape)
        buf("s_" + kind, L if kind in SUMS_TWICE else 1, *four, *shape)
        buf("x_" + kind, copies, *four, *shape)
        if spread:
            buf("y_" + kind, copies, 3, *shape)
        buf("z_" + kind, copies, 3, *quarter(shape))
        buf("p_" + kind, copies, *quarter(shape))
        buf("h_" + kind, copies, *quarter(shape))
    named["send"] = pltpu.SemaphoreType.DMA((SEMS,))
    named["recv"] = pltpu.SemaphoreType.DMA((SEMS,))
    named["local"] = pltpu.SemaphoreType.DMA((LOCAL_SEMS,))
    named["credit"] = pltpu.SemaphoreType.REGULAR((8,))
    return named


SEMS = 266
LOCAL_SEMS = 53
INPUTS = ("tokens", "cotangent", "lengths", "gain_one", "gain_two", "wq", "wk", "wv", "wo", "wg", "wu", "wd")
OUTPUTS = ("out_act", "out_grad", "f_m", "f_o", "f_q", "f_kv", "hq", "hk", "hv", "ho", "hm")


class Refs:
    pass


def step_kernel(*refs):
    R = Refs()
    names = INPUTS + OUTPUTS + tuple(scratch_shapes())
    for name, ref in zip(names, refs, strict=True):
        setattr(R, name, ref)
    x_hi, z, core, y, x_lo = coords()
    sems = (R.send, R.recv)
    slots = Slots()
    local_slots = Slots()
    spread_at = [slots.take(4) for _ in range(4)]
    back_at = [slots.take(4) for _ in range(4)]
    kept_slots = slots.used
    sibling = device(x_hi, z, 1 - core, y, x_lo)
    near = [device(x_hi, z, core, y, 1 - x_lo), device(1 - x_hi, z, core, y, 1 - x_lo)]
    far = device(1 - x_hi, z, core, y, x_lo)

    def along_y(k):
        return device(x_hi, z, core, (y + k) % 4, x_lo)

    def along_z(k):
        return device(x_hi, (z + k) % 4, core, y, x_lo)

    barrier = pltpu.get_barrier_semaphore()
    everyone = [along_y(k) for k in (1, 2, 3)] + [along_z(k) for k in (1, 2, 3)]
    everyone += near + [far, sibling]
    for target in everyone:
        pl.semaphore_signal(barrier, inc=1, device_id=target, device_id_type=MESH)
    pl.semaphore_wait(barrier, len(everyone))
    home = core == x_lo
    guest = jnp.logical_not(home)

    def keep(src, dst):
        return pltpu.make_async_copy(src, dst, R.local.at[local_slots.take()])

    def start_all(copies):
        for copy in copies:
            copy.start()

    def wait_all(copies):
        for copy in copies:
            copy.wait()

    slab_weights = [
        (R.wq, (R.aq, R.hq), 0),
        (R.wk, (R.ak, R.hk), 1),
        (R.wv, (R.av, R.hv), 1),
        (R.wo, (R.ao, R.ho), None),
    ]
    own_copy, ring, cross, swap, first_swap = {}, {}, {}, {}, {}
    for l in range(LAYERS):
        for a, (src, (here, there), side) in enumerate(slab_weights):
            dst = here if l == 0 else there.at[1]
            if l == 0:
                own_copy[a] = keep(src.at[l], dst.at[y, core])
            for k in (1, 2, 3):
                ring[l, a, k] = remote(src.at[l], dst.at[y, core], sems, slots.take(), along_y(k))
            for k in range(4):
                at = dst.at[(y - k + 4) % 4, core]
                to = near[(0, 0, 1, 1)[k] if side is None else 1 if side == 0 and k == 2 else side]
                cross[l, a, k] = remote(src.at[l] if k == 0 else at, at, sems, slots.take(), to)
                slot = slots.take()
                swap[l, a, k] = remote(at, at, sems, slot, sibling)
                if k == 0:
                    first_swap[l, a] = remote(src.at[l], at, sems, slot, sibling)
    QKV, OUT, ALL = (0, 1, 2), (3,), (0, 1, 2, 3)
    PLANES = (((0, 1), (3, 1)), ((0, 2), (3, 2)), ((0, 3), (3, 3)), tuple((a, k) for a in (1, 2) for k in (1, 2, 3)))
    ring_z = {}
    for units in PLANES:
        for a, k in units:
            at = slab_weights[a][1][1].at[1, (y - k + 4) % 4, core]
            for m in (1, 2, 3):
                ring_z[a, k, m] = remote(at, at, sems, slots.take(), along_z(m))

    def by_plane(body):
        for plane in range(4):

            @pl.when(jnp.logical_and(home, z == plane))
            def _():
                body(plane)

    def planes_begin():
        @pl.when(home)
        def _():
            for a in ALL:
                cross[1, a, 0].start()
                first_swap[1, a].start()

        def body(plane):
            for a, k in PLANES[plane]:
                ring[1, a, k].start()

        by_plane(body)

    def planes_z():
        def body(plane):
            for a, k in PLANES[plane]:
                ring[1, a, k].wait_recv()
                for m in (1, 3, 2):
                    ring_z[a, k, m].start()
                cross[1, a, k].start()
                swap[1, a, k].start()

        by_plane(body)

    def planes_pass():
        def body(plane):
            for other in (3, 0, 1, 2):
                if other != plane:
                    for a, k in PLANES[other]:
                        ring_z[a, k, (plane - other) % 4].wait_recv()
                        cross[1, a, k].start()
                        swap[1, a, k].start()

        by_plane(body)

    def planes_sent():
        def body(plane):
            for a, k in PLANES[plane]:
                ring[1, a, k].wait_send()
                for m in (1, 2, 3):
                    ring_z[a, k, m].wait_send()

        by_plane(body)

    def gather_begin(l, arrays):
        @pl.when(home)
        def _():
            for a in arrays:
                for k in ORDER_Y:
                    ring[l, a, k].start()
                cross[l, a, 0].start()
                first_swap[l, a].start()
                if l == 0:
                    own_copy[a].start()

    def gather_home(l, arrays):
        @pl.when(home)
        def _():
            for k in ORDER_Y:
                for a in arrays:
                    ring[l, a, k].wait_recv()
                    cross[l, a, k].start()
                    swap[l, a, k].start()

    def gather_guest(l, arrays):
        @pl.when(guest)
        def _():
            for k in (0,) + ORDER_Y:
                for a in arrays:
                    cross[l, a, k].wait_recv()
                    swap[l, a, k].start()

    def gather_end(l, arrays):
        for a in arrays:
            for k in range(4):
                swap[l, a, k].wait_recv()
        if l == 0:

            @pl.when(home)
            def _():
                for a in arrays:
                    own_copy[a].wait()

    def gather_sent(l, arrays):
        for a in arrays:

            @pl.when(home)
            def _():
                if l == 0:
                    for k in (1, 2, 3):
                        ring[l, a, k].wait_send()
                for k in range(4):
                    cross[l, a, k].wait_send()

            for k in range(4):
                swap[l, a, k].wait_send()

    saves = [keep(here, there.at[0]) for _, (here, there), _ in slab_weights]
    load_back = [keep(there.at[0], here) for _, (here, there), _ in slab_weights]
    load_own, load_core, load_rest = [], [], []
    for src, (here, there), _ in slab_weights:
        slot = local_slots.take()
        at = here.at[y, core]
        load_own.append(pltpu.make_async_copy(src.at[1], at, R.local.at[slot]))
        load_core.append(pltpu.make_async_copy(there.at[1, y, core], at, R.local.at[slot]))
        rest = [keep(there.at[1, y, 1 - core], here.at[y, 1 - core])]
        for k in (1, 2, 3):
            rest.append(keep(there.at[1, (y + k) % 4], here.at[(y + k) % 4]))
        load_rest.append(rest)

    def load_begin(arrays):
        for a in arrays:
            start_all(load_rest[a])

        @pl.when(home)
        def _():
            start_all([load_own[a] for a in arrays])

        @pl.when(guest)
        def _():
            start_all([load_core[a] for a in arrays])

    def load_end(arrays):
        for a in arrays:
            wait_all(load_rest[a])
            load_own[a].wait()

    mlp_in = [R.wg, R.wu, R.wd]
    save_m = keep(R.mw.at[1 - x_lo], R.hm.at[0])
    load_m = [
        [keep(R.hm.at[l], R.mw.at[1 - x_lo])]
        + [keep(mlp_in[a].at[l], R.mw.at[x_lo, a]) for a in range(3)]
        for l in range(LAYERS)
    ]

    own_gain, other_gain = R.all_gains.at[y, x_lo], R.all_gains.at[y, 1 - x_lo]
    gain_keep = keep(R.own_gains, own_gain)
    gain_x = remote(R.own_gains, own_gain, sems, slots.take(), near[0])
    gain_y = [remote(R.own_gains, own_gain, sems, slots.take(), along_y(k)) for k in (1, 2, 3)]
    gain_pass = [remote(other_gain, other_gain, sems, slots.take(), along_y(k)) for k in (1, 2, 3)]

    SIZES = ((0, 48), (48, 32))
    cross_m, ring_m, pass_m, keep_m = {}, {}, {}, {}
    slot_cross = {(l, a): slots.take() for l in range(LAYERS) for a in range(3)}
    slot_ring = {(l, k): slots.take() for l in range(LAYERS) for k in (1, 2, 3)}
    slot_pass = {(l, k): slots.take() for l in range(LAYERS) for k in range(4)}
    for l in range(LAYERS):
        there_m = R.mw.at[x_lo] if l == 0 else R.hm.at[1]
        here_m = R.mw.at[1 - x_lo] if l == 0 else R.hm.at[1]
        if l == 0:
            for a in range(3):
                keep_m[a] = keep(mlp_in[a].at[l], R.mw.at[x_lo, a])
        for c, (first, size) in enumerate(SIZES):

            def rows(where):
                return pl.ds(pl.multiple_of(where * (FFS // 4) + first, 16), size)

            for a in range(3):
                cross_m[l, c, a] = remote(
                    mlp_in[a].at[l, rows(z)], there_m.at[a, rows(z)], sems, slot_cross[l, a], near[c]
                )
            for k in range(4):
                at = here_m.at[:, rows((z - k + 4) % 4)]
                pass_m[l, c, k] = remote(at, at, sems, slot_pass[l, k], sibling)
            for k in (1, 2, 3):
                at = here_m.at[:, rows(z)]
                ring_m[l, c, k] = remote(at, at, sems, slot_ring[l, k], along_z(k))

    def by_core(body):
        for c in range(2):

            @pl.when(core == c)
            def _():
                body(c)

    def pairs_begin(l):
        def body(c):
            for a in range(3):
                cross_m[l, c, a].start()

        by_core(body)
        if l == 0:
            start_all(keep_m.values())

    def pairs_z(l):
        def body(c):
            for a in range(3):
                cross_m[l, c, a].wait_recv()
            for k in ORDER_Y:
                ring_m[l, c, k].start()
            pass_m[l, c, 0].start()

        by_core(body)

    def pairs_pass(l):
        def body(c):
            for k in ORDER_Y:
                ring_m[l, c, k].wait_recv()
                pass_m[l, c, k].start()

        by_core(body)

    def pairs_end(l):
        def body(c):
            for k in range(4):
                pass_m[l, 1 - c, k].wait_recv()

        by_core(body)
        if l == 0:
            wait_all(keep_m.values())

    def pairs_sent(l):
        def body(c):
            for a in range(3):
                cross_m[l, c, a].wait_send()
            for k in (1, 2, 3):
                ring_m[l, c, k].wait_send()
            for k in range(4):
                pass_m[l, c, k].wait_send()

        by_core(body)


    def spread_copy(n, buffer, k):
        return remote(buffer.at[y], buffer.at[y], sems, spread_at[n] + k, along_y(k))

    def spread(n, buffer, targets=ORDER_Y):
        for k in targets:
            spread_copy(n, buffer, k).start()

    def arrived(n, buffer, k):
        there = buffer.at[(y - k + 4) % 4]
        remote(there, there, sems, spread_at[n] + k, along_y(k)).wait_recv()

    def back_copy(n, k):
        return remote(
            R.parts.at[int(n == 1), k - 1], R.came.at[int(n == 1), k - 1], sems, back_at[n] + k, along_y(4 - k)
        )

    def collect(n, total):
        for k in ORDER_Y:
            back_copy(n, k).wait_recv()
            total = total + R.came[int(n == 1), k - 1].astype(F32)
        return total

    def back(n):
        for k in ORDER_Y:
            back_copy(n, k).start()

    def sent(n, buffer):
        for k in (1, 2, 3):
            spread_copy(n, buffer, k).wait_send()

    def sent_back(n):
        for k in (1, 2, 3):
            back_copy(n, k).wait_send()

    reds = {}
    credit_at = {"m": 0, "o": 4}

    def give(kind, which, targets):
        for target in targets:
            pl.semaphore_signal(
                R.credit.at[credit_at[kind] + which], inc=1, device_id=target, device_id_type=MESH
            )

    def take(kind, which, count):
        pl.semaphore_wait(R.credit.at[credit_at[kind] + which], count)

    class Reduction:
        def __init__(self, kind, l):
            self.kind, self.l = kind, l
            shape, self.spread = KINDS[kind]
            self.planes, self.rows = shape[0], shape[1]
            self.b = b = l if kind in TWICE else 0
            self.gives = kind in credit_at and l == 1
            self.takes = kind in credit_at and l == 0
            self.g = R.g_q if kind == "o" else getattr(R, "g_" + kind)
            self.s = getattr(R, "s_" + kind).at[l if kind in SUMS_TWICE else 0]
            self.x = getattr(R, "x_" + kind).at[b]
            self.zb = getattr(R, "z_" + kind).at[b]
            self.p = getattr(R, "p_" + kind).at[b]
            self.h = getattr(R, "h_" + kind).at[b]
            self.f = getattr(R, "f_" + kind).at[l]
            self.chunk = {128: 64, 320: 80}[self.rows]
            n = 4 if self.spread else 1
            self.at_pair = slots.take(n)
            self.at_x = slots.take(4 if self.spread else 2)
            self.at_y = slots.take(4)
            self.at_z = slots.take(4)
            self.at_out = slots.take(4)
            self.at_far = slots.take()
            self.at_last = slots.take()
            self.own = pltpu.make_async_copy(self.p, self.piece(self.f, z), R.local.at[local_slots.take()])
            if self.spread:
                self.yb = getattr(R, "y_" + kind).at[b]

        def piece(self, ref, where):
            size = self.rows // 4
            return ref.at[:, pl.ds(pl.multiple_of(where * size, 16), size)]

        def add(self, dst, others, chunk=None):
            for i in range(self.planes):
                accumulate(dst.at[i], [o.at[i] for o in others], chunk or self.chunk)

        def pair(self, q):
            if self.spread:
                return remote(self.g.at[q, 1 - core], self.s.at[q], sems, self.at_pair + q, sibling)
            return remote(self.g.at[1 - core], self.s, sems, self.at_pair, sibling)

        def over_x(self, q):
            if self.spread:
                return remote(self.s.at[q], self.x.at[q], sems, self.at_x + q, near[q // 2])
            half = slice(q * (self.rows // 2), (q + 1) * (self.rows // 2))
            return remote(self.s.at[:, half], self.x.at[:, half], sems, self.at_x + q, near[q])

        def came_x(self, q):
            return remote(self.s.at[q], self.x.at[q], sems, self.at_x + q, near[0])

        def over_y(self, k):
            return remote(self.s.at[(y + k) % 4], self.yb.at[k - 1], sems, self.at_y + k, along_y(k))

        def mine(self):
            return self.s.at[y] if self.spread else self.s

        def over_z(self, k):
            return remote(
                self.piece(self.mine(), (z + k) % 4), self.zb.at[k - 1], sems, self.at_z + k, along_z(k)
            )

        def over_far(self):
            return remote(self.p, self.h, sems, self.at_far, far)

        def out_z(self, k):
            return remote(self.p, self.piece(self.f, z), sems, self.at_out + k, along_z(k))

        def last(self):
            return remote(self.f, self.f, sems, self.at_last, sibling)

        def begin(self):
            if self.takes and self.kind == "m":
                take(self.kind, 0, 1)
            for q in (0, 2, 1, 3) if self.spread else (0,):
                self.pair(q).start()

        def step_x(self):
            if self.takes:
                self.when_guest(lambda: take(self.kind, 1, 2))
            for q in (0, 2, 1, 3) if self.spread else (0,):
                self.pair(q).wait()
                if self.spread:
                    self.add(self.s.at[q], [self.g.at[q, core]])
                    self.when_guest(lambda: self.over_x(q).start())
                else:
                    self.add(self.s, [self.g.at[core]])
                    self.when_guest(lambda: [self.over_x(i).start() for i in range(2)])

        def step_y(self):
            @pl.when(home)
            def _():
                if self.spread:
                    if self.takes:
                        take(self.kind, 0, 3)
                    for k in ORDER_Y + (0,):
                        q = (y + k) % 4
                        self.came_x(q).wait_recv()
                        self.add(self.s.at[q], [self.x.at[q]])
                        if k:
                            self.over_y(k).start()
                else:
                    for q in range(2):
                        self.over_x(q).wait_recv()
                    self.add(self.s, [self.x])
                    self.start_z()
                if self.gives:
                    give(self.kind, 1, near)

        def start_z(self):
            if self.takes:
                take(self.kind, 2, 3)
            for k in ORDER_Y:
                self.over_z(k).start()

        def step_z(self):
            if self.spread:

                @pl.when(home)
                def _():
                    for k in ORDER_Y:
                        self.over_y(k).wait_recv()
                    self.add(self.mine(), [self.yb.at[j] for j in range(3)])
                    if self.gives:
                        give(self.kind, 0, [along_y(k) for k in (1, 2, 3)])
                    self.start_z()

        def step_far(self):
            @pl.when(home)
            def _():
                for k in ORDER_Y:
                    self.over_z(k).wait_recv()
                for i in range(self.planes):
                    total = self.piece(self.mine(), z)[i].astype(F32)
                    for j in range(3):
                        total = total + self.zb[j, i].astype(F32)
                    self.p[i] = total.astype(BF)
                if self.takes:
                    take(self.kind, 3, 1)
                self.over_far().start()
                for k in (1, 2, 3):
                    self.over_z(k).wait_send()
                    if self.spread:
                        self.over_y(k).wait_send()
                if self.gives:
                    give(self.kind, 2, [along_z(k) for k in (1, 2, 3)])

            @pl.when(guest)
            def _():
                for q in range(4 if self.spread else 2):
                    self.over_x(q).wait_send()

            if self.gives and self.kind == "m":
                give(self.kind, 0, [sibling])

        def step_out(self):
            @pl.when(home)
            def _():
                self.over_far().wait()
                self.add(self.p, [self.h], self.rows // 4)
                self.own.start()
                for k in ORDER_Y:
                    self.out_z(k).start()
                if self.gives:
                    give(self.kind, 3, [far])

        def step_last(self):
            @pl.when(home)
            def _():
                self.own.wait()
                for k in ORDER_Y:
                    self.out_z(k).wait()
                self.last().start()

        def finish(self):
            @pl.when(home)
            def _():
                self.last().wait_send()

            @pl.when(guest)
            def _():
                self.last().wait_recv()

        def when_guest(self, body):
            @pl.when(guest)
            def _():
                body()

    first_slots = slots
    for l in (1, 0):
        if l == 0:
            slots = Slots()
            slots.take(kept_slots)
        for kind in KINDS:
            reds[kind, l] = Reduction(kind, l)

    assert max(slots.used, first_slots.used) <= SEMS and local_slots.used <= LOCAL_SEMS

    column = lax.broadcasted_iota(jnp.int32, (ROWS, PAD), 1)
    first_half = column % HEAD < HEAD // 2

    def turn(block, sign):
        ahead = pltpu.roll(block, PAD - HEAD // 2, 1)
        behind = pltpu.roll(block, HEAD // 2, 1)
        return jnp.where(first_half, -sign * ahead, sign * behind)

    def rotated(block):
        return block * R.cosine[...] + turn(block, 1.0) * R.sine[...]

    def rotated_back(block):
        return block * R.cosine[...] + turn(block * R.sine[...], -1.0)

    def inverse_rms(x):
        return lax.rsqrt(jnp.mean(x * x, axis=-1, keepdims=True) + norm_eps)

    def head_lanes(h):
        return slice(h * HEAD, (h + 1) * HEAD)

    def tables():
        one, two = R.lengths[0, 0], R.lengths[0, 1]
        row = lax.broadcasted_iota(jnp.int32, (ROWS, PAD), 0)

        def doc(t):
            return (t >= one).astype(jnp.int32) + (t >= one + two).astype(jnp.int32)

        own = doc(row)
        begins = jnp.where(own == 0, 0, jnp.where(own == 1, one, one + two))
        allowed = jnp.logical_and(own == doc(column), column <= row)
        R.bias[...] = jnp.where(allowed, 0.0, masked_value)
        slow = jnp.exp((column % (HEAD // 2)).astype(F32) * (-2.0 * log_base / HEAD))
        angles = (row - begins).astype(F32) * slow
        R.cosine[...] = jnp.cos(angles)
        R.sine[...] = jnp.sin(angles)
        wide_column = lax.broadcasted_iota(jnp.int32, (D, 8 * PAD), 1)
        wide_row = lax.broadcasted_iota(jnp.int32, (D, 8 * PAD), 0)
        lane = wide_column % PAD
        R.place[...] = jnp.where(
            jnp.logical_and(lane < SHARD, (wide_column // PAD) * SHARD + lane == wide_row), 1.0, 0.0
        ).astype(BF)
        R.wide[...] = jnp.zeros_like(R.wide)
        R.narrow[...] = jnp.zeros_like(R.narrow)
        R.gain_rows[...] = jnp.zeros_like(R.gain_rows)
        R.stream[0] = R.tokens[...].astype(F32).T

    def soft_weights(l, kv):
        rows = jnp.concatenate([R.qrot[l, :, head_lanes(kv * SHARE + i)] for i in range(SHARE)], axis=0)
        keys = R.krot[l, :, head_lanes(kv)]
        scores = dot_t(rows, keys) * score_scale
        scores = scores + jnp.concatenate([R.bias[...]] * SHARE, axis=0)
        weights = jnp.exp(scores - jnp.max(scores, axis=-1, keepdims=True))
        return rows, keys, weights / jnp.sum(weights, axis=-1, keepdims=True)

    def attention_forward(l, ready_qkv, ready_out):
        x = R.stream[l]
        normed = (x * inverse_rms(x) * R.gain_full[l : l + 1, :]).astype(BF)
        R.npad[l] = dot(normed, R.place[...]).astype(BF)

        def project(weights, width, product):
            total = jnp.zeros((ROWS, width), F32)
            for g in range(8):
                total = total + product(
                    R.npad[l, :, g * PAD : g * PAD + SHARD], weights[g // 2, g % 2]
                )
            return total

        ready_qkv()
        R.wide[:, :D] = project(R.aq, D, dot)
        R.narrow[:, :KV] = project(R.ak, KV, dot_t)
        R.vals[l, :, :KV] = project(R.av, KV, dot_t).astype(BF)
        for j in range(8):
            at = slice(j * PAD, (j + 1) * PAD)
            R.qrot[l, :, at] = rotated(R.wide[:, at]).astype(BF)
        for j in range(3):
            at = slice(j * PAD, (j + 1) * PAD)
            R.krot[l, :, at] = rotated(R.narrow[:, at]).astype(BF)
        for kv in range(KV_HEADS):
            rows, keys, soft = soft_weights(l, kv)
            out = dot(soft.astype(BF), R.vals[l, :, head_lanes(kv)]).astype(BF)
            for i in range(SHARE):
                R.gproj_q[:, head_lanes(kv * SHARE + i)] = out[i * ROWS : (i + 1) * ROWS]
        R.mpad[l] = dot(R.gproj_q[:, :D], R.place[...]).astype(BF)
        ready_out()
        total = x
        for g in range(8):
            total = total + dot(R.mpad[l, :, g * PAD : g * PAD + SHARD], R.ao[g // 2, g % 2])
        R.hidden[l] = total
        R.acts_in[l, y] = (total * inverse_rms(total) * R.gain_full[2 + l : 3 + l, :]).astype(BF)

    def blocks(n, buffer, body, between=None):
        def block(i, carry):
            k = order(i)
            b = (y - k + 4) % 4
            if between is not None:
                pl.when(i == 1)(between)

            @pl.when(i > 0)
            def _():
                arrived(n, buffer, k)

            total = body(b)
            if total is None:
                return carry

            @pl.when(i == 0)
            def _():
                R.own_part[...] = total

            @pl.when(i > 0)
            def _():
                R.parts[int(n == 1), k - 1] = total.astype(BF)
                back_copy(n, k).start()

            return carry

        lax.fori_loop(0, 4, block, 0)

    def mlp_forward(l, n, down=True, between=None):
        def body(b):
            rows = R.acts_in[l, b]
            total = jnp.zeros((ROWS, D), F32) if down else None
            for p in range(2):
                gate = dot_t(rows, R.mw[p, 0])
                up = dot_t(rows, R.mw[p, 1])
                act = (gate * jax.nn.sigmoid(gate) * up).astype(BF)
                R.s_gate[l, p, b] = gate.astype(BF)
                R.s_up[l, p, b] = up.astype(BF)
                R.s_act[l, p, b] = act
                if down:
                    total = total + dot(act, R.mw[p, 2])
            return total

        blocks(n, R.acts_in.at[l], body, between)

    def mlp_down(l, n):
        def block(i, carry):
            k = order(i)
            b = (y - k + 4) % 4
            total = dot(R.s_act[l, 0, b], R.mw[0, 2]) + dot(R.s_act[l, 1, b], R.mw[1, 2])

            @pl.when(i == 0)
            def _():
                R.out_grad[...] = (total + R.hidden[l]).T

            @pl.when(i > 0)
            def _():
                R.parts[int(n == 1), k - 1] = total.astype(BF)

            return carry

        lax.fori_loop(0, 4, block, 0)

    def result_out(n):
        R.out_act[...] = (R.out_grad[...] + collect(n, jnp.zeros((ROWS, D), F32)).T).astype(BF)

    def mlp_backward(l, n):
        def body(b):
            rows = R.grads_in[1 - l, b]
            total = jnp.zeros((ROWS, D), F32)
            for p in range(2):
                grad_active = dot_t(rows, R.mw[p, 2])
                gate = R.s_gate[l, p, b].astype(F32)
                up = R.s_up[l, p, b].astype(F32)
                sig = jax.nn.sigmoid(gate)
                grad_gate = (grad_active * up * sig * (1.0 + gate * (1.0 - sig))).astype(BF)
                grad_up = (grad_active * gate * sig).astype(BF)
                R.s_gate[l, p, b] = grad_gate
                R.s_up[l, p, b] = grad_up
                total = total + dot(grad_gate, R.mw[p, 0]) + dot(grad_up, R.mw[p, 1])
            return total

        blocks(n, R.grads_in.at[1 - l], body)

    def mlp_grads(l):
        def grads(p, carry):
            ins = R.acts_in[l].reshape(4 * ROWS, D)
            R.g_m[p, 0] = t_dot(R.s_gate[l, p].reshape(4 * ROWS, FFS), ins).astype(BF)
            R.g_m[p, 1] = t_dot(R.s_up[l, p].reshape(4 * ROWS, FFS), ins).astype(BF)
            R.g_m[p, 2] = t_dot(
                R.s_act[l, p].reshape(4 * ROWS, FFS), R.grads_in[1 - l].reshape(4 * ROWS, D)
            ).astype(BF)
            return carry

        lax.fori_loop(0, 2, grads, 0)

    def slab_loop(body):
        def run(g, carry):
            body(g, g // 2, g % 2)
            return carry

        lax.fori_loop(0, 8, run, 0)

    def norm_back(x, grad_normed, gain_row):
        r = inverse_rms(x)
        u = grad_normed * gain_row
        back = r * u - x * (r * r * r) * jnp.mean(u * x, axis=-1, keepdims=True)
        return back, jnp.sum(grad_normed * x * r, axis=0, keepdims=True)

    def back_hidden(l, n):
        grad_input = collect(n, R.own_part[...])
        back, grad_gain = norm_back(R.hidden[l], grad_input, R.gain_full[2 + l : 3 + l, :])
        grad_hidden = R.grad[...] + back
        R.grad[...] = grad_hidden
        R.glow[...] = grad_hidden.astype(BF)
        R.gain_rows[1:2, :] = grad_gain

        def back_out(g, h, i):
            R.wide[:, lanes(g, SHARD)] = dot_t(R.glow[...], R.ao[h, i])

        slab_loop(back_out)
        R.gmix[...] = dot_t(R.wide[...].astype(BF), R.place[...]).astype(BF)

    def grads_out(l):
        def body(g, h, i):
            R.g_q[h, i, 0] = t_dot(R.mpad[l, :, lanes(g, PAD)], R.glow[...]).astype(BF)

        slab_loop(body)

    def back_heads(l):
        for kv in range(KV_HEADS):
            rows, keys, soft = soft_weights(l, kv)
            heads = [kv * SHARE + i for i in range(SHARE)]
            gm = jnp.concatenate([R.gmix[:, head_lanes(h)] for h in heads], axis=0)
            grad_probs = dot_t(gm, R.vals[l, :, head_lanes(kv)])
            inner = jnp.sum(soft * grad_probs, axis=-1, keepdims=True)
            grad_scores = (soft * (grad_probs - inner)).astype(BF)
            grad_rows = dot(grad_scores, keys) * score_scale
            for i, h in enumerate(heads):
                R.wide[:, head_lanes(h)] = grad_rows[i * ROWS : (i + 1) * ROWS]
            R.narrow[:, head_lanes(kv)] = t_dot(grad_scores, rows) * score_scale
            R.gproj_v[:, head_lanes(kv)] = t_dot(soft.astype(BF), gm).astype(BF)
        for j in range(8):
            at = slice(j * PAD, (j + 1) * PAD)
            R.gproj_q[:, at] = rotated_back(R.wide[:, at]).astype(BF)
        for j in range(3):
            at = slice(j * PAD, (j + 1) * PAD)
            R.gproj_k[:, at] = rotated_back(R.narrow[:, at]).astype(BF)

    def back_stream(l):
        def back_in(g, h, i):
            R.wide[:, lanes(g, SHARD)] = (
                dot_t(R.gproj_q[:, :D], R.aq[h, i])
                + dot(R.gproj_k[:, :KV], R.ak[h, i])
                + dot(R.gproj_v[:, :KV], R.av[h, i])
            )

        slab_loop(back_in)
        high, low = halves(R.wide[...])
        grad_normed = dot_t(high, R.place[...]) + dot_t(low, R.place[...])
        back, grad_gain = norm_back(R.stream[l], grad_normed, R.gain_full[l : l + 1, :])
        R.grad[...] = R.grad[...] + back
        R.gain_rows[0:1, :] = grad_gain

    def grads_kv(l):
        def body(g, h, i):
            right = R.npad[l, :, lanes(g, PAD)]
            R.g_kv[h, i, 0] = t_dot(R.gproj_k[:, :KV], right).astype(BF)
            R.g_kv[h, i, 1] = t_dot(R.gproj_v[:, :KV], right).astype(BF)

        slab_loop(body)

    def grads_q(l):
        high, low = halves(R.gain_rows[...])
        R.gain_grad[...] = dot(high, R.place[...]) + dot(low, R.place[...])

        def body(g, h, i):
            total = t_dot(R.npad[l, :, lanes(g, PAD)], R.gproj_q[:, :D])
            rows = lax.broadcasted_iota(jnp.int32, (PAD, PAD), 0)
            corner = (
                total[:, :PAD]
                + jnp.where(rows == SHARD, R.gain_grad[0:1, lanes(g, PAD)], 0.0)
                + jnp.where(rows == SHARD + 1, R.gain_grad[1:2, lanes(g, PAD)], 0.0)
            )
            R.g_q[h, i, 0] = total.astype(BF)
            R.g_q[h, i, 0, :, :PAD] = corner.astype(BF)

        slab_loop(body)

    gather_begin(0, QKV)
    R.own_gains[...] = jnp.zeros_like(R.own_gains)
    R.own_gains[0:2, :SHARD] = R.gain_one[...]
    R.own_gains[2:4, :SHARD] = R.gain_two[...]
    gain_keep.start()
    gain_x.start()
    start_all(gain_y)
    pairs_begin(0)
    gather_home(0, QKV)
    gather_begin(0, OUT)
    planes_begin()
    tables()
    gain_x.wait()
    start_all(gain_pass)
    gather_guest(0, QKV)
    pairs_z(0)
    gather_home(0, OUT)
    gain_keep.wait()
    wait_all(gain_y)
    wait_all(gain_pass)
    for g in range(8):
        R.gain_pad[:, g * PAD : (g + 1) * PAD] = R.all_gains[g // 2, g % 2]
    R.gain_full[...] = dot_t(R.gain_pad[...], R.place[...])
    gather_guest(0, OUT)
    pairs_begin(1)

    def ready_out():
        gather_end(0, OUT)
        pairs_pass(0)
        planes_z()
        start_all(saves)

    attention_forward(0, lambda: gather_end(0, QKV), ready_out)
    spread(0, R.acts_in.at[0])
    pairs_end(0)
    save_m.start()

    def between():
        planes_pass()
        pairs_z(1)

    mlp_forward(0, 0, between=between)
    gather_guest(1, QKV)
    gather_sent(0, ALL)
    wait_all(saves)
    pairs_pass(1)
    cot = R.cotangent[...].astype(F32).T
    R.grads_in[0, y] = cot.astype(BF)
    R.grad[...] = cot
    gather_end(1, QKV)
    load_begin(QKV)
    R.stream[1] = collect(0, R.own_part[...] + R.hidden[0])
    spread(2, R.grads_in.at[0], (1, 3))
    pairs_sent(0)
    save_m.wait()
    gather_guest(1, OUT)

    def ready_out_1():
        gather_end(1, OUT)
        load_begin(OUT)
        pairs_end(1)
        start_all(load_m[1])
        load_end(OUT)

    attention_forward(1, lambda: load_end(QKV), ready_out_1)
    spread(1, R.acts_in.at[1])
    spread(2, R.grads_in.at[0], (2,))
    sent(0, R.acts_in.at[0])
    sent_back(0)
    wait_all(load_m[1])
    mlp_forward(1, 1, down=False)

    m1, o1, q1, kv1 = (reds[kind, 1] for kind in ("m", "o", "q", "kv"))
    m0, o0, q0, kv0 = (reds[kind, 0] for kind in ("m", "o", "q", "kv"))
    mlp_backward(1, 2)
    mlp_grads(1)
    gather_sent(1, ALL)
    planes_sent()
    pairs_sent(1)
    m1.begin()
    mlp_down(1, 1)
    start_all(load_m[0])
    back_hidden(1, 2)
    back(1)
    m1.step_x()
    back_heads(1)
    back_stream(1)
    R.grads_in[1, y] = R.grad[...].astype(BF)
    spread(3, R.grads_in.at[1])
    start_all(load_back)
    grads_out(1)
    o1.begin()
    grads_kv(1)
    kv1.begin()
    result_out(1)
    o1.step_x()
    m1.step_y()
    grads_q(1)
    q1.begin()
    sent(1, R.acts_in.at[1])
    sent_back(2)
    wait_all(load_m[0])
    mlp_backward(0, 3)
    kv1.step_x()
    q1.step_x()
    mlp_grads(0)
    m1.step_far()
    m0.begin()
    o1.step_y()
    wait_all(load_back)
    back_hidden(0, 3)
    m0.step_x()
    grads_out(0)
    o0.begin()
    kv1.step_y()
    q1.step_y()
    o1.step_z()
    m1.step_out()
    back_heads(0)
    o0.step_x()
    grads_kv(0)
    kv0.begin()
    kv1.step_z()
    q1.step_z()
    m0.step_y()
    back_stream(0)
    kv0.step_x()
    grads_q(0)
    q0.begin()
    o1.step_far()
    R.out_grad[...] = R.grad[...].T
    o0.step_y()
    q0.step_x()
    m1.step_last()
    m0.step_far()
    kv0.step_y()
    kv1.step_far()
    q1.step_far()
    o1.step_out()
    o0.step_z()
    kv0.step_z()
    q0.step_y()
    kv1.step_out()
    q1.step_out()
    o1.step_last()
    o0.step_far()
    kv0.step_far()
    q0.step_z()
    m0.step_out()
    o0.step_out()
    kv0.step_out()
    q0.step_far()
    kv1.step_last()
    q1.step_last()
    q0.step_out()
    o0.step_last()
    kv0.step_last()
    m0.step_last()
    q0.step_last()
    for red in (m1, o1, kv1, q1, m0, kv0, o0, q0):
        red.finish()
    sent(2, R.grads_in.at[0])
    sent(3, R.grads_in.at[1])
    sent_back(1)
    sent_back(3)


def step(*args):
    L = LAYERS

    def out(*shape, dtype=BF):
        return jax.ShapeDtypeStruct(shape, dtype)

    return pl.pallas_call(
        step_kernel,
        out_shape=(
            out(D, ROWS),
            out(D, ROWS, dtype=F32),
            out(L, 3, FFS, D),
            out(L, 1, ROWS, D),
            out(L, 1, ROWS, D),
            out(L, 2, KV, PAD),
            out(L, 4, 2, SHARD, D),
            out(L, 4, 2, KV, SHARD),
            out(L, 4, 2, KV, SHARD),
            out(L, 4, 2, SHARD, D),
            out(L, 3, FFS, D),
        ),
        in_specs=[VMEM] * 2 + [SMEM] + [VMEM] * 2 + [ANY] * 7,
        out_specs=[VMEM] * 2 + [ANY] * 9,
        scratch_shapes=list(scratch_shapes().values()),
        compiler_params=pltpu.CompilerParams(
            collective_id=1, has_side_effects=True, vmem_limit_bytes=63 * 2**20
        ),
    )(*args)


def widen_kernel(
    act, grad, fm, fo, fq, fkv,
    act_out, grad_out, gate, up, down, out, query, key, value, gain_one, gain_two,
    act_v, grad_v, fm_v, fo_v, fq_v, fkv_v, m_w, o_w, q_w, k_w, v_w, came, went,
):
    ins = [pltpu.make_async_copy(fm.at[l], fm_v.at[l], came.at[l]) for l in range(LAYERS)]
    rest = ((fq, fq_v), (fo, fo_v), (fkv, fkv_v), (act, act_v), (grad, grad_v))
    ins += [pltpu.make_async_copy(src, dst, came.at[2 + i]) for i, (src, dst) in enumerate(rest)]
    for copy in ins:
        copy.start()
    outs = []

    def put(src, dst):
        outs.append(pltpu.make_async_copy(src, dst, went.at[len(outs)]))
        outs[-1].start()

    for l in range(LAYERS):
        ins[l].wait()
        for a, dst in enumerate((gate, up, down)):
            m_w[l, a] = fm_v[l, a].astype(F32)
            put(m_w.at[l, a], dst.at[l])
    for copy in ins[2:]:
        copy.wait()
    put(act_v, act_out)
    put(grad_v, grad_out)
    for l in range(LAYERS):
        wide = fq_v[l, 0].astype(F32)
        q_w[l] = wide[:SHARD]
        gain_one[l : l + 1, :] = wide[SHARD : SHARD + 1, :SHARD]
        gain_two[l : l + 1, :] = wide[SHARD + 1 : SHARD + 2, :SHARD]
    put(q_w, query)
    o_w[...] = fo_v[:, 0, :SHARD].astype(F32)
    put(o_w, out)
    k_w[...] = fkv_v[:, 0, :, :SHARD].astype(F32)
    put(k_w, key)
    v_w[...] = fkv_v[:, 1, :, :SHARD].astype(F32)
    put(v_w, value)
    for copy in outs:
        copy.wait()


def widen(act, grad, fm, fo, fq, fkv):
    L = LAYERS

    def out(*shape):
        return jax.ShapeDtypeStruct(shape, F32)

    ins = (act, grad, fm, fo, fq, fkv)
    wide = ((L, 3, FFS, D), (L, SHARD, D), (L, SHARD, D), (L, KV, SHARD), (L, KV, SHARD))
    return pl.pallas_call(
        widen_kernel,
        out_shape=(
            jax.ShapeDtypeStruct(act.shape, act.dtype), out(*grad.shape),
            out(L, FFS, D), out(L, FFS, D), out(L, FFS, D), out(L, SHARD, D), out(L, SHARD, D),
            out(L, KV, SHARD), out(L, KV, SHARD), out(L, SHARD), out(L, SHARD),
        ),
        in_specs=[ANY] * 6,
        out_specs=[ANY] * 9 + [VMEM] * 2,
        scratch_shapes=[pltpu.VMEM(a.shape, a.dtype) for a in ins]
        + [pltpu.VMEM(shape, F32) for shape in wide]
        + [pltpu.SemaphoreType.DMA((7,)), pltpu.SemaphoreType.DMA((12,))],
        compiler_params=pltpu.CompilerParams(vmem_limit_bytes=63 * 2**20),
    )(*ins)


def shards(
    tokens, cotangent, lengths, gain_attn, w_query, w_key, w_value, w_out, gain_mlp, w_gate, w_up, w_down
):
    def turned(a):
        return jnp.swapaxes(a, -1, -2)

    act, grad, fm, fo, fq, fkv, *_ = step(
        turned(tokens), turned(cotangent), lengths, gain_attn, gain_mlp,
        w_query, turned(w_key), turned(w_value), w_out, turned(w_gate), turned(w_up), w_down,
    )
    act, grad, gate, up, down, out, query, key, value, gain_one, gain_two = widen(
        act, grad, fm, fo, fq, fkv
    )
    return (
        turned(act),
        turned(grad),
        gain_one,
        query,
        turned(key),
        turned(value),
        out,
        gain_two,
        turned(gate),
        turned(up),
        down,
    )


def solution(mesh):
    in_specs = (
        P(("replica", "group"), None),
        P(("replica", "group"), None),
        P(("replica", "group"), None),
        P(None, "group"),
        P(None, "group", None),
        P(None, "group", None),
        P(None, "group", None),
        P(None, "group", None),
        P(None, "group"),
        P(None, None, "group"),
        P(None, None, "group"),
        P(None, "group", None),
    )
    out_specs = (
        P(("replica", "group"), None),
        P(("replica", "group"), None),
        P(None, "group"),
        P(None, "group", None),
        P(None, "group", None),
        P(None, "group", None),
        P(None, "group", None),
        P(None, "group"),
        P(None, None, "group"),
        P(None, None, "group"),
        P(None, "group", None),
    )
    return jax.shard_map(shards, mesh=mesh, in_specs=in_specs, out_specs=out_specs, check_vma=False)
```

profile of v0, /device:TPU:1, one launch (start us, length us, event | category | flops | bytes accessed | tf_op | source)
XLA Modules:
  0.0 253.5 jit_solution(10948824901321915256)
XLA Ops:
  0.6 246.1 %shard_map.203 = (bf16[960,128]{1,0:T(8,128)(2,1)}, f32[960,128]{1,0:T(8,128)}, bf16[2,3,320,960]{3,2,1,0:T(8,128)(2,1)}, bf16[2,1,128,960]{3,2,1,0:T(8,128)(2,1...) custom-call(bf16[960,128]{1,0:T(8,128)(2,1)} %bitcast.14, ...), custom_call_target="tpu_custom_call" | custom-call | tf_op jit(solution)/shard_map/pallas_call | solution.py:1187
  246.7 6.5 %shard_map.204 = (bf16[960,128]{1,0:T(8,128)(2,1)}, f32[960,128]{1,0:T(8,128)}, f32[2,320,960]{2,1,0:T(8,128)}, f32[2,320,960]{2,1,0:T(8,128)}, f32[2,320,960]{2...) custom-call(bf16[960,128]{1,0:T(8,128)(2,1)} %get-tuple-element.28.a, ...), custom_call_target="tpu_custom_call" | custom-call | tf_op jit(solution)/shard_map/pallas_call | solution.py:1260
where the time goes:
time: 258 us; the launch traced here: 253 us
  Pallas kernels  253 us (98%)
    pallas_call x1, Pallas kernels, step(): pl.pallas_call(step_kernel, out_shape=(out(D, ROWS), out(D, ROWS, dtype=F...  246 us
    pallas_call x1, Pallas kernels, widen(): pl.pallas_call(widen_kernel, out_shape=(jax.ShapeDtypeStruct(act.shape, a...  6.52 us

commit v1 on v0

--- a/solution.py
+++ b/solution.py
@@ -176,7 +176,7 @@
     return named
 
 
-SEMS = 266
+SEMS = 274
 LOCAL_SEMS = 53
 INPUTS = ("tokens", "cotangent", "lengths", "gain_one", "gain_two", "wq", "wk", "wv", "wo", "wg", "wu", "wd")
 OUTPUTS = ("out_act", "out_grad", "f_m", "f_o", "f_q", "f_kv", "hq", "hk", "hv", "ho", "hm")
@@ -556,7 +556,7 @@
             self.at_x = slots.take(4 if self.spread else 2)
             self.at_y = slots.take(4)
             self.at_z = slots.take(4)
-            self.at_out = slots.take(4)
+            self.at_out = slots.take(4 * self.planes if kind == "m" else 4)
             self.at_far = slots.take()
             self.at_last = slots.take()
             self.own = pltpu.make_async_copy(self.p, self.piece(self.f, z), R.local.at[local_slots.take()])
@@ -601,6 +601,15 @@
 
         def out_z(self, k):
             return remote(self.p, self.piece(self.f, z), sems, self.at_out + k, along_z(k))
+
+        def out_z_plane(self, k, i):
+            src, dst = self.p.at[i], self.piece(self.f, z).at[i]
+            return remote(src, dst, sems, self.at_out + 4 * i + k, along_z(k))
+
+        def outs(self, planes=None):
+            if self.spread:
+                return [self.out_z(k) for k in ORDER_Y]
+            return [self.out_z_plane(k, i) for i in planes or range(self.planes) for k in ORDER_Y]
 
         def last(self):
             return remote(self.f, self.f, sems, self.at_last, sibling)
@@ -689,14 +698,13 @@
             if self.gives and self.kind == "m":
                 give(self.kind, 0, [sibling])
 
-        def step_out(self):
+        def step_out(self, planes=None):
             @pl.when(home)
             def _():
                 self.over_far().wait()
                 self.add(self.p, [self.h], self.rows // 4)
                 self.own.start()
-                for k in ORDER_Y:
-                    self.out_z(k).start()
+                start_all(self.outs(planes))
                 if self.gives:
                     give(self.kind, 3, [far])
 
@@ -704,9 +712,13 @@
             @pl.when(home)
             def _():
                 self.own.wait()
-                for k in ORDER_Y:
-                    self.out_z(k).wait()
+                wait_all(self.outs())
                 self.last().start()
+
+        def step_out_rest(self, planes):
+            @pl.when(home)
+            def _():
+                start_all(self.outs(planes))
 
         def finish(self):
             @pl.when(home)
@@ -827,7 +839,7 @@
             k = order(i)
             b = (y - k + 4) % 4
             if between is not None:
-                pl.when(i == 1)(between)
+                pl.when(i == 3)(between)
 
             @pl.when(i > 0)
             def _():
@@ -1022,6 +1034,9 @@
     gather_home(0, QKV)
     gather_begin(0, OUT)
     planes_begin()
+    cot = R.cotangent[...].astype(F32).T
+    R.grads_in[0, y] = cot.astype(BF)
+    R.grad[...] = cot
     tables()
     gain_x.wait()
     start_all(gain_pass)
@@ -1056,14 +1071,11 @@
     gather_guest(1, QKV)
     gather_sent(0, ALL)
     wait_all(saves)
-    pairs_pass(1)
-    cot = R.cotangent[...].astype(F32).T
-    R.grads_in[0, y] = cot.astype(BF)
-    R.grad[...] = cot
     gather_end(1, QKV)
     load_begin(QKV)
     R.stream[1] = collect(0, R.own_part[...] + R.hidden[0])
     spread(2, R.grads_in.at[0], (1, 3))
+    pairs_pass(1)
     pairs_sent(0)
     save_m.wait()
     gather_guest(1, OUT)
@@ -1157,9 +1169,10 @@
     q1.step_out()
     o1.step_last()
     o0.step_far()
+    m0.step_out((0,))
     kv0.step_far()
     q0.step_z()
-    m0.step_out()
+    m0.step_out_rest((1, 2))
     o0.step_out()
     kv0.step_out()
     q0.step_far()

time: 258 us -> 254 us (0.984)
  Pallas kernels: 253 us -> 249 us
    pallas_call x1, Pallas kernels: 246 us -> 242 us  [step(): pl.pallas_call(step_kernel, out_shape=(out(D, ROWS), out(D, ROWS, dtype=F...]
where the time goes in v1:
time: 254 us; the launch traced here: 250 us
  Pallas kernels  249 us (98%)
    pallas_call x1, Pallas kernels, step(): pl.pallas_call(step_kernel, out_shape=(out(D, ROWS), out(D, ROWS, dtype=F...  242 us
    pallas_call x1, Pallas kernels, widen(): pl.pallas_call(widen_kernel, out_shape=(jax.ShapeDtypeStruct(act.shape, a...  6.52 us

profile of v1, /device:TPU:1, one launch (start us, length us, event | category | flops | bytes accessed | tf_op | source)
XLA Modules:
  0.0 249.7 jit_solution(10773522036676481393)
XLA Ops:
  0.6 242.3 %shard_map.203 = (bf16[960,128]{1,0:T(8,128)(2,1)}, f32[960,128]{1,0:T(8,128)}, bf16[2,3,320,960]{3,2,1,0:T(8,128)(2,1)}, bf16[2,1,128,960]{3,2,1,0:T(8,128)(2,1...) custom-call(bf16[960,128]{1,0:T(8,128)(2,1)} %bitcast.14, ...), custom_call_target="tpu_custom_call" | custom-call | tf_op jit(solution)/shard_map/pallas_call | solution.py:1200
  243.0 6.5 %shard_map.204 = (bf16[960,128]{1,0:T(8,128)(2,1)}, f32[960,128]{1,0:T(8,128)}, f32[2,320,960]{2,1,0:T(8,128)}, f32[2,320,960]{2,1,0:T(8,128)}, f32[2,320,960]{2...) custom-call(bf16[960,128]{1,0:T(8,128)(2,1)} %get-tuple-element.28.a, ...), custom_call_target="tpu_custom_call" | custom-call | tf_op jit(solution)/shard_map/pallas_call | solution.py:1273
